TPU v7x, 32 devices: a whole 2x2x4 slice. The times are simulated.
32 devices in a mesh: grp: 4 (over z), dev: 8 (over y, x, core).
Axes of the slice: x: 2, y: 2, z: 4, core: 2. Of those that a mesh axis runs over, the one named last changes fastest.
Arguments:
- positions: float32 [3, 32768], P(None, ('grp', 'dev')), may hold values from -3 to 3
- velocities: float32 [3, 32768], P(None, ('grp', 'dev')), may hold values from -5 to 5
- accelerations: float32 [3, 32768], P(None, ('grp', 'dev')), may hold values from -3 to 3
- jerks: float32 [3, 32768], P(None, ('grp', 'dev')), may hold values from -3 to 3
- levels: int32 [32768], P(('grp', 'dev')), may hold values from 0 to 5
- counts: int32 [2, 32], replicated, may hold values from 1 to 256, 4096 in all within a row
- active_rows: int32 [2, 8192], P(None, ('grp', 'dev')), may hold values from 0 to 1023, as said below
Outputs:
- new_positions: float32 [3, 32768], P(None, ('grp', 'dev'))
- new_velocities: float32 [3, 32768], P(None, ('grp', 'dev'))
- new_accelerations: float32 [3, 32768], P(None, ('grp', 'dev'))
- new_jerks: float32 [3, 32768], P(None, ('grp', 'dev'))
Inputs may be any that keep to these rules, and one draw needn't show every extreme that they name: In each step the 32 counts sum to exactly 4096 and the largest of them is exactly 256. `active_rows`: for each step and device, the 256 entries of the device's slots are distinct indices of that device's own stars; only the first counts of them are live.
All inputs are finite; a program needn't handle non-finite values.
Results may differ from a plain program's by a relative error of at most 0.00022.
Values sent between devices are 32-bit elements; how exact they have to be, the bound alone decides.
A program may use at most 128 MiB of HBM per device.

v0:
```python
import math

import jax
import jax.numpy as jnp
from jax import lax
from jax.sharding import PartitionSpec as P

tick_length = 1.0 / 128.0


def pair_block(targets, src_pos, src_vel, mass, soft_sq):
    gap_x = src_pos[0][None, :] - targets[0][:, None]
    gap_y = src_pos[1][None, :] - targets[1][:, None]
    gap_z = src_pos[2][None, :] - targets[2][:, None]
    drift_x = src_vel[0][None, :] - targets[3][:, None]
    drift_y = src_vel[1][None, :] - targets[4][:, None]
    drift_z = src_vel[2][None, :] - targets[5][:, None]
    squared = gap_x * gap_x + gap_y * gap_y + gap_z * gap_z + soft_sq
    inverse = lax.rsqrt(squared)
    weight = mass * inverse * inverse * inverse
    along = 3.0 * (gap_x * drift_x + gap_y * drift_y + gap_z * drift_z) * inverse * inverse
    return jnp.stack(
        [
            jnp.sum(weight * gap_x, axis=1),
            jnp.sum(weight * gap_y, axis=1),
            jnp.sum(weight * gap_z, axis=1),
            jnp.sum(weight * (drift_x - along * gap_x), axis=1),
            jnp.sum(weight * (drift_y - along * gap_y), axis=1),
            jnp.sum(weight * (drift_z - along * gap_z), axis=1),
        ]
    )


def block_terms(packed, src_pos, src_vel, mass, soft_sq):
    width, total = packed.shape
    block = math.gcd(total, 2048)
    grouped = packed.reshape(width, total // block, block).transpose(1, 0, 2)
    result = lax.map(lambda targets: pair_block(targets, src_pos, src_vel, mass, soft_sq), grouped)
    return result.transpose(1, 0, 2).reshape(width, total)


def predict(positions, velocities, accelerations, jerks, elapsed):
    span = elapsed[None, :]
    pred_pos = (
        positions
        + span * velocities
        + 0.5 * span * span * accelerations
        + span * span * span / 6.0 * jerks
    )
    pred_vel = velocities + span * accelerations + 0.5 * span * span * jerks
    return (pred_pos, pred_vel)


def correct(old_pos, old_vel, old_acc, old_jerk, force, jerk_new, span):
    span = span[None, :]
    new_vel = old_vel + 0.5 * span * (old_acc + force) + span * span / 12.0 * (old_jerk - jerk_new)
    new_pos = old_pos + 0.5 * span * (old_vel + new_vel) + span * span / 12.0 * (old_acc - force)
    return (new_pos, new_vel)


def shards(positions, velocities, accelerations, jerks, levels, counts, active_rows):
    devices_all = lax.axis_size("grp") * lax.axis_size("dev")
    my_rank = lax.axis_index("grp") * lax.axis_size("dev") + lax.axis_index("dev")
    star_dev = positions.shape[1]
    slot_cap = active_rows.shape[1]
    stars_all = star_dev * devices_all
    mass = 1.0 / stars_all
    soft_sq = 0.0004 * (131072.0 / stars_all) ** (2.0 / 3.0)
    last_time = -(jnp.left_shift(jnp.int32(1), levels) - 1).astype(jnp.float32) * tick_length
    for step in range(active_rows.shape[0]):
        now = (step + 1) * tick_length
        pred_pos, pred_vel = predict(positions, velocities, accelerations, jerks, now - last_time)
        rows = active_rows[step]
        targets = jnp.concatenate([pred_pos[:, rows], pred_vel[:, rows]], axis=0)
        step_counts = counts[step]
        own_count = step_counts[my_rank]
        gathered = lax.all_gather(targets[None], ("grp", "dev"), axis=0, tiled=True)
        flat = gathered.transpose(1, 0, 2).reshape(6, devices_all * slot_cap)
        terms = block_terms(flat, pred_pos, pred_vel, mass, soft_sq)
        totals = lax.psum(terms, ("grp", "dev"))
        own = lax.dynamic_slice_in_dim(totals, my_rank * slot_cap, slot_cap, 1)
        span = now - last_time[rows]
        new_pos, new_vel = correct(
            positions[:, rows],
            velocities[:, rows],
            accelerations[:, rows],
            jerks[:, rows],
            own[:3],
            own[3:],
            span,
        )
        live = jnp.arange(slot_cap, dtype=jnp.int32) < own_count
        target = jnp.where(live, rows, star_dev)
        positions = positions.at[:, target].set(new_pos, mode="drop")
        velocities = velocities.at[:, target].set(new_vel, mode="drop")
        accelerations = accelerations.at[:, target].set(own[:3], mode="drop")
        jerks = jerks.at[:, target].set(own[3:], mode="drop")
        last_time = last_time.at[target].set(now, mode="drop")
    return (positions, velocities, accelerations, jerks)


def solution(mesh):
    placed = (
        P(None, ("grp", "dev")),
        P(None, ("grp", "dev")),
        P(None, ("grp", "dev")),
        P(None, ("grp", "dev")),
        P(("grp", "dev")),
        P(),
        P(None, ("grp", "dev")),
    )
    return jax.shard_map(
        shards,
        mesh=mesh,
        in_specs=placed,
        out_specs=(
            P(None, ("grp", "dev")),
            P(None, ("grp", "dev")),
            P(None, ("grp", "dev")),
            P(None, ("grp", "dev")),
        ),
        check_vma=False,
    )
```

profile of v0, /device:TPU:0, one launch (start us, length us, event | category | flops | bytes accessed | tf_op | source)
XLA Modules:
  0.0 500.4 jit_solution(2783241706770817821)
XLA Ops:
  7.2 0.8 fusion.58
  8.6 2.1 compare_select_fusion
  10.6 0.7 negate_multiply_fusion
  11.3 0.8 multiply_add_fusion.2
  12.3 0.7 gather_fusion.4
  13.4 0.7 gather_fusion.5
  14.2 43.9 %all-gather.2 = f32[32,6,256]{2,1,0:T(8,128)S(1)} all-gather(f32[1,6,256]{2,1,0:T(8,128)S(1)} %maximum_bitcast_fusion), channel_id=2, replica_groups=mesh['grp'=4,'dev'=8] {'grp','dev'}, dimensions={0}, use_global_device_ids=true | all-gather | bytes 202752 | tf_op jit(solution)/shard_map/all_gather | solution.py:77
  58.2 65.7 %while.20 = (s32[]{:T(128)}, f32[4,6,2048]{2,1,0:T(8,128)S(1)}, f32[3,1024]{1,0:T(4,128)S(1)}, f32[4,6,2048]{2,1,0:T(8,128)S(1)}, f32[3,1024]{1,0:T(4,128)S(1)},...) while((s32[]{:T(128)}, f32[4,6,2048]{2,1,0:T(8,128)S(1)}, ...), condition=%wide.region_7.8_spmd, body=%wide.region_0.7_spmd.sunk | while | flops 85970952 | bytes 499917 | solution.py:38
  58.3 16.2 %fusion.64 = (f32[2048]{0:T(1024)S(1)}, f32[2048]{0:T(1024)S(1)}, f32[2048]{0:T(1024)S(1)}, f32[2048]{0:T(1024)S(1)}, f32[2048]{0:T(1024)S(1)}, /*index=5*/f32[2048]{0:T(1024)S(1)}) fusion(f32[2048]{0:T(1024)S(1)} %bitcast.257, f32[1024]{0:T(1024)S(1)} %bitcast.269, f32[2048]{0:T(1024)S(1)} %bitcast.254, f32[1024]{0:T(1024)S(1)} %bitcast.272, ...), kind=kLoop, calls=%fused_computation.45.clone.1 | loop fusion | flops 85970944 | bytes 122880 | tf_op jit(solution)/shard_map/while/body/eval_jaxpr/reduce_sum | solution.py:29
  74.7 16.2 %fusion.64 = (f32[2048]{0:T(1024)S(1)}, f32[2048]{0:T(1024)S(1)}, f32[2048]{0:T(1024)S(1)}, f32[2048]{0:T(1024)S(1)}, f32[2048]{0:T(1024)S(1)}, /*index=5*/f32[2048]{0:T(1024)S(1)}) fusion(f32[2048]{0:T(1024)S(1)} %bitcast.257, f32[1024]{0:T(1024)S(1)} %bitcast.269, f32[2048]{0:T(1024)S(1)} %bitcast.254, f32[1024]{0:T(1024)S(1)} %bitcast.272, ...), kind=kLoop, calls=%fused_computation.45.clone.1 | loop fusion | flops 85970944 | bytes 122880 | tf_op jit(solution)/shard_map/while/body/eval_jaxpr/reduce_sum | solution.py:29
  91.1 16.2 %fusion.64 = (f32[2048]{0:T(1024)S(1)}, f32[2048]{0:T(1024)S(1)}, f32[2048]{0:T(1024)S(1)}, f32[2048]{0:T(1024)S(1)}, f32[2048]{0:T(1024)S(1)}, /*index=5*/f32[2048]{0:T(1024)S(1)}) fusion(f32[2048]{0:T(1024)S(1)} %bitcast.257, f32[1024]{0:T(1024)S(1)} %bitcast.269, f32[2048]{0:T(1024)S(1)} %bitcast.254, f32[1024]{0:T(1024)S(1)} %bitcast.272, ...), kind=kLoop, calls=%fused_computation.45.clone.1 | loop fusion | flops 85970944 | bytes 122880 | tf_op jit(solution)/shard_map/while/body/eval_jaxpr/reduce_sum | solution.py:29
  107.6 16.2 %fusion.64 = (f32[2048]{0:T(1024)S(1)}, f32[2048]{0:T(1024)S(1)}, f32[2048]{0:T(1024)S(1)}, f32[2048]{0:T(1024)S(1)}, f32[2048]{0:T(1024)S(1)}, /*index=5*/f32[2048]{0:T(1024)S(1)}) fusion(f32[2048]{0:T(1024)S(1)} %bitcast.257, f32[1024]{0:T(1024)S(1)} %bitcast.269, f32[2048]{0:T(1024)S(1)} %bitcast.254, f32[1024]{0:T(1024)S(1)} %bitcast.272, ...), kind=kLoop, calls=%fused_computation.45.clone.1 | loop fusion | flops 85970944 | bytes 122880 | tf_op jit(solution)/shard_map/while/body/eval_jaxpr/reduce_sum | solution.py:29
  125.9 1.4 gather_fusion.1
  127.3 0.7 gather_fusion
  128.1 0.7 gather_fusion.2
  128.9 0.7 gather_fusion.3
  129.7 0.7 gather_fusion.6
  130.5 1.4 scatter_fusion.1
  132.0 1.4 gather_fusion.8
  133.3 112.6 %all-reduce.3.cloned.1.call-done = f32[6,8192]{1,0:T(8,128)} async-done(((f32[6,8192]{1,0:T(8,128)}), f32[6,8192]{1,0:T(8,128)}) %all-reduce.3.cloned.1.call-update) | async-done | bytes 196624 | tf_op jit(solution)/shard_map/psum | solution.py:80
  245.9 0.9 fusion.47
  246.9 1.4 scatter_fusion.2
  248.4 1.4 scatter_fusion.3
  250.0 1.4 scatter_fusion.4
  251.5 1.4 scatter_fusion
  253.3 0.7 gather_fusion.11
  254.3 0.7 gather_fusion.12
  255.4 40.5 %all-gather.3 = f32[32,6,256]{2,1,0:T(8,128)S(1)} all-gather(f32[1,6,256]{2,1,0:T(8,128)S(1)} %maximum_bitcast_fusion.1), channel_id=3, replica_groups=mesh['grp'=4,'dev'=8] {'grp','dev'}, dimensions={0}, use_global_device_ids=true | all-gather | bytes 202752 | tf_op jit(solution)/shard_map/all_gather | solution.py:77
  295.8 65.6 %while.21 = (s32[]{:T(128)}, f32[4,6,2048]{2,1,0:T(8,128)S(1)}, f32[3,1024]{1,0:T(4,128)S(1)}, f32[4,6,2048]{2,1,0:T(8,128)S(1)}, f32[3,1024]{1,0:T(4,128)S(1)},...) while((s32[]{:T(128)}, f32[4,6,2048]{2,1,0:T(8,128)S(1)}, ...), condition=%wide.region_21.22_spmd, body=%wide.region_14.21_spmd.sunk | while | flops 85970952 | bytes 499917 | solution.py:38
  296.0 16.2 %fusion.66 = (f32[2048]{0:T(1024)S(1)}, f32[2048]{0:T(1024)S(1)}, f32[2048]{0:T(1024)S(1)}, f32[2048]{0:T(1024)S(1)}, f32[2048]{0:T(1024)S(1)}, /*index=5*/f32[2048]{0:T(1024)S(1)}) fusion(f32[2048]{0:T(1024)S(1)} %bitcast.263, f32[1024]{0:T(1024)S(1)} %bitcast.275, f32[2048]{0:T(1024)S(1)} %bitcast.260, f32[1024]{0:T(1024)S(1)} %bitcast.278, ...), kind=kLoop, calls=%fused_computation.85.clone.1 | loop fusion | flops 85970944 | bytes 122880 | tf_op jit(solution)/shard_map/while/body/eval_jaxpr/reduce_sum | solution.py:29
  312.3 16.2 %fusion.66 = (f32[2048]{0:T(1024)S(1)}, f32[2048]{0:T(1024)S(1)}, f32[2048]{0:T(1024)S(1)}, f32[2048]{0:T(1024)S(1)}, f32[2048]{0:T(1024)S(1)}, /*index=5*/f32[2048]{0:T(1024)S(1)}) fusion(f32[2048]{0:T(1024)S(1)} %bitcast.263, f32[1024]{0:T(1024)S(1)} %bitcast.275, f32[2048]{0:T(1024)S(1)} %bitcast.260, f32[1024]{0:T(1024)S(1)} %bitcast.278, ...), kind=kLoop, calls=%fused_computation.85.clone.1 | loop fusion | flops 85970944 | bytes 122880 | tf_op jit(solution)/shard_map/while/body/eval_jaxpr/reduce_sum | solution.py:29
  328.7 16.2 %fusion.66 = (f32[2048]{0:T(1024)S(1)}, f32[2048]{0:T(1024)S(1)}, f32[2048]{0:T(1024)S(1)}, f32[2048]{0:T(1024)S(1)}, f32[2048]{0:T(1024)S(1)}, /*index=5*/f32[2048]{0:T(1024)S(1)}) fusion(f32[2048]{0:T(1024)S(1)} %bitcast.263, f32[1024]{0:T(1024)S(1)} %bitcast.275, f32[2048]{0:T(1024)S(1)} %bitcast.260, f32[1024]{0:T(1024)S(1)} %bitcast.278, ...), kind=kLoop, calls=%fused_computation.85.clone.1 | loop fusion | flops 85970944 | bytes 122880 | tf_op jit(solution)/shard_map/while/body/eval_jaxpr/reduce_sum | solution.py:29
  345.1 16.2 %fusion.66 = (f32[2048]{0:T(1024)S(1)}, f32[2048]{0:T(1024)S(1)}, f32[2048]{0:T(1024)S(1)}, f32[2048]{0:T(1024)S(1)}, f32[2048]{0:T(1024)S(1)}, /*index=5*/f32[2048]{0:T(1024)S(1)}) fusion(f32[2048]{0:T(1024)S(1)} %bitcast.263, f32[1024]{0:T(1024)S(1)} %bitcast.275, f32[2048]{0:T(1024)S(1)} %bitcast.260, f32[1024]{0:T(1024)S(1)} %bitcast.278, ...), kind=kLoop, calls=%fused_computation.85.clone.1 | loop fusion | flops 85970944 | bytes 122880 | tf_op jit(solution)/shard_map/while/body/eval_jaxpr/reduce_sum | solution.py:29
  361.4 0.7 copy-done
  362.1 0.7 gather_fusion.9
  362.9 0.7 gather_fusion.10
  363.6 0.7 gather_fusion.13
  364.3 0.7 gather_fusion.7
  365.4 118.0 %all-reduce.5.cloned.1.call-done = f32[6,8192]{1,0:T(8,128)} async-done(((f32[6,8192]{1,0:T(8,128)}), f32[6,8192]{1,0:T(8,128)}) %all-reduce.5.cloned.1.call-update) | async-done | bytes 196624 | tf_op jit(solution)/shard_map/psum | solution.py:80
  483.4 0.9 fusion.38
  484.4 1.4 scatter_fusion.8
  485.8 0.8 copy.178
  486.8 1.4 scatter_fusion.7
  488.1 0.8 copy.177
  489.1 1.4 scatter_fusion.6
  490.4 0.8 copy.176
  491.4 1.4 scatter_fusion.5
  492.8 0.8 copy.175
  (87 shorter events, 7.3 us)
Async XLA Ops:
  7.2 238.8 %all-reduce.3.cloned.1.call-start = ((), (), s32[]{:S(2)}) async-start(), calls=%async_computation | async-start | bytes 524288 | tf_op jit(solution)/shard_map/psum | solution.py:80
  58.2 66.5 %copy-start.2 = (f32[3,1024]{1,0:T(4,128)S(1)}, f32[3,1024]{1,0:T(4,128)}, u32[]{:S(2)}) copy-start(f32[3,1024]{1,0:T(4,128)} %param.11) | copy-start | bytes 36868
  123.9 0.7 copy-start.1
  123.9 1.0 copy-start.3
  124.6 0.7 copy-start.4
  124.6 358.8 %all-reduce.5.cloned.1.call-start = ((), (), s32[]{:S(2)}) async-start(), calls=%async_computation.1 | async-start | bytes 524288 | tf_op jit(solution)/shard_map/psum | solution.py:80
  124.9 0.7 copy-start.5
  361.4 0.7 copy-start
Sparse Core Ops, SparseCore 0:
  124.7 121.1 all-reduce.2
  362.3 121.1 all-reduce.4
where the time goes:
time: 501 us; the launch traced here: 500 us
  waiting for transfers between devices  231 us (46%)
  other arithmetic  135 us (27%)
  blocking collectives  84.4 us (17%)
  local copies, waits for them, and re-layouts  35.3 us (7%)
  between operations  14.4 us (3%)
    psum x2, waiting for transfers between devices, shards(): totals = lax.psum(terms, ('grp', 'dev'))  231 us
    reduce_sum x8, other arithmetic, pair_block(): jnp.sum(weight * (drift_z - along * gap_z), axis=1)  129 us
    all_gather x2, blocking collectives, shards(): gathered = lax.all_gather(targets[None], ('grp', 'dev'), axis=0, tiled=True)  84.4 us
  transfers between devices with their start and end apart: 2, of which 2 were waited for; matrix products, arithmetic and copies ran while one was open for 2% of the time, Pallas kernels for 0%

commit v1 on v0

v1 whole, which is shorter than its diff:
```python
import functools

import jax
import jax.numpy as jnp
from jax import lax
from jax.experimental import pallas as pl
from jax.experimental.pallas import tpu as pltpu
from jax.sharding import PartitionSpec as P

tick_length = 1.0 / 128.0
COLS = 256
ROWS = 128
F32 = jnp.float32
BF16 = jnp.bfloat16
NT = (((1,), (1,)), ((), ()))


def split3(value):
    high = value.astype(BF16).astype(F32)
    rest = value - high
    middle = rest.astype(BF16).astype(F32)
    return high, middle, rest - middle


def accumulate(chunk, width, slots, left_ref, place_ref, pairs_ref, total_ref):
    for start in range(0, width, COLS):
        source = chunk[:, start : start + COLS]
        high, middle, low = split3(source)
        right = jnp.concatenate([high, high, high, middle, middle, low], axis=0).astype(BF16)
        parts = jnp.concatenate([high, middle, low, jnp.zeros_like(low)], axis=0).astype(BF16)
        for row in range(0, slots, ROWS):
            rows = slice(row, row + ROWS)
            mixed = jnp.dot(left_ref[rows, :], right, preferred_element_type=F32)
            for lane in range(0, COLS, 128):
                lanes = slice(lane, lane + 128)
                gap_x = source[0:1, lanes] - place_ref[0, rows, :]
                gap_y = source[1:2, lanes] - place_ref[1, rows, :]
                gap_z = source[2:3, lanes] - place_ref[2, rows, :]
                squared = gap_x * gap_x + gap_y * gap_y + gap_z * gap_z + place_ref[3, 0:1, :]
                inverse = lax.rsqrt(squared)
                twice = inverse * inverse
                weight = twice * inverse
                along = weight * twice * mixed[:, lanes]
                weight_high = weight.astype(BF16)
                along_high = along.astype(BF16)
                pairs_ref[0, rows, lanes] = weight_high
                pairs_ref[1, rows, lanes] = (weight - weight_high.astype(F32)).astype(BF16)
                pairs_ref[2, rows, lanes] = along_high
                pairs_ref[3, rows, lanes] = (along - along_high.astype(F32)).astype(BF16)
        total_ref[0:32, :] += lax.dot_general(
            parts, pairs_ref[0], NT, preferred_element_type=F32
        ) + lax.dot_general(parts, pairs_ref[1], NT, preferred_element_type=F32)
        total_ref[32:64, :] += lax.dot_general(
            parts, pairs_ref[2], NT, preferred_element_type=F32
        ) + lax.dot_general(parts, pairs_ref[3], NT, preferred_element_type=F32)


def kernel(
    groups,
    peers,
    steps,
    soft_sq,
    mass,
    positions,
    velocities,
    accelerations,
    jerks,
    levels,
    counts,
    active_rows,
    out_pos,
    out_vel,
    out_acc,
    out_jerk,
    held,
    state,
    picked,
    left,
    place,
    pairs,
    total,
    send_sem,
    recv_sem,
):
    stars = positions.shape[1]
    slots = active_rows.shape[1]
    grp = lax.axis_index("grp")
    dev = lax.axis_index("dev")
    me = grp * peers + dev

    barrier = pltpu.get_barrier_semaphore()
    for ahead in range(1, groups):
        pl.semaphore_signal(
            barrier, inc=1, device_id=(lax.rem(grp + ahead, groups), dev),
            device_id_type=pl.DeviceIdType.MESH,
        )
    for ahead in range(1, peers):
        pl.semaphore_signal(
            barrier, inc=1, device_id=(grp, lax.rem(dev + ahead, peers)),
            device_id_type=pl.DeviceIdType.MESH,
        )

    state[0:3, :] = positions[...]
    state[3:6, :] = velocities[...]
    state[6:9, :] = accelerations[...]
    state[9:12, :] = jerks[...]
    state[12:13, :] = -(jnp.left_shift(jnp.int32(1), levels[...]) - 1).astype(F32) * tick_length
    state[13:16, :] = jnp.zeros((3, stars), F32)
    place[3] = jnp.full((slots, 128), soft_sq, F32)

    def send(step, owner, lane, target):
        return pltpu.make_async_remote_copy(
            src_ref=held.at[step, owner],
            dst_ref=held.at[step, owner],
            send_sem=send_sem.at[step, lane],
            recv_sem=recv_sem.at[step, owner],
            device_id=target,
            device_id_type=pl.DeviceIdType.MESH,
        )

    def group_copy(step, ahead):
        return send(step, me, ahead - 1, (lax.rem(grp + ahead, groups), dev))

    def peer_copy(step, back, ahead):
        owner = lax.rem(grp + groups - back, groups) * peers + dev
        lane = (groups - 1) + back * (peers - 1) + ahead - 1
        return send(step, owner, lane, (grp, lax.rem(dev + ahead, peers)))

    def one_step(step, carry):
        now = (step + 1).astype(F32) * tick_length
        span = now - state[12:13, :]
        pred_pos = (
            state[0:3, :]
            + span * state[3:6, :]
            + 0.5 * span * span * state[6:9, :]
            + span * span * span / 6.0 * state[9:12, :]
        )
        pred_vel = state[3:6, :] + span * state[6:9, :] + 0.5 * span * span * state[9:12, :]
        held[step, me, 0:3, :] = pred_pos
        held[step, me, 3:6, :] = pred_vel
        held[step, me, 6:7, :] = jnp.sum(pred_pos * pred_vel, axis=0, keepdims=True)
        held[step, me, 7:8, :] = jnp.ones((1, stars), F32)

        @pl.when(step == 0)
        def _():
            pl.semaphore_wait(barrier, groups + peers - 2)

        for ahead in range(1, groups):
            group_copy(step, ahead).start()
        for ahead in range(1, peers):
            peer_copy(step, 0, ahead).start()

        rows = active_rows[pl.ds(step, 1), :]
        chosen = lax.broadcasted_iota(jnp.int32, (stars, slots), 0) == rows
        chosen = jnp.where(chosen, 1.0, 0.0).astype(BF16)
        values = jnp.concatenate([held[step, me], state[...]], axis=0)
        pieces = jnp.concatenate(split3(values), axis=0).astype(BF16)
        found = jnp.dot(pieces, chosen, preferred_element_type=F32)
        found = found[0:24] + (found[24:48] + found[48:72])
        picked[...] = found
        moved = jnp.concatenate(
            [-found[3:6], -found[0:3], jnp.ones((1, slots), F32), found[6:7]], axis=0
        )
        high, middle, low = split3(moved)
        side = jnp.concatenate(
            [high, middle, low, high, middle, high, found[0:8], jnp.zeros((72, slots), F32)], axis=0
        ).T
        left[...] = side[:, 0:48].astype(BF16)
        for axis in range(3):
            place[axis] = jnp.broadcast_to(side[:, 48 + axis : 49 + axis], (slots, 128))
        total[...] = jnp.zeros_like(total)

        def one_chunk(turn, inner):
            owner_grp = lax.rem(grp + groups - lax.rem(turn, groups), groups)
            owner_dev = lax.rem(dev + peers - turn // groups, peers)
            owner = owner_grp * peers + owner_dev

            @pl.when(turn == 1)
            def _():
                for back in range(1, groups):
                    sender = lax.rem(grp + groups - back, groups) * peers + dev
                    send(step, sender, 0, (grp, lax.rem(dev + 1, peers))).wait_recv()
                    for ahead in range(1, peers):
                        peer_copy(step, back, ahead).start()

            @pl.when(turn >= groups)
            def _():
                send(step, owner, 0, (grp, lax.rem(dev + 1, peers))).wait_recv()

            accumulate(held[step, owner], stars, slots, left, place, pairs, total)
            return inner

        lax.fori_loop(0, groups * peers, one_chunk, 0)

        for ahead in range(1, groups):
            group_copy(step, ahead).wait_send()
        for back in range(groups):
            for ahead in range(1, peers):
                peer_copy(step, back, ahead).wait_send()

        sums = total[...]
        direct = sums[0:8] + (sums[8:16] + sums[16:24])
        turned = sums[32:40] + (sums[40:48] + sums[48:56])
        pred = picked[0:8, :]
        force = mass * (direct[0:3] - pred[0:3] * direct[7:8])
        jerk = mass * (
            (direct[3:6] - pred[3:6] * direct[7:8]) - 3.0 * (turned[0:3] - pred[0:3] * turned[7:8])
        )
        old_pos, old_vel = picked[8:11, :], picked[11:14, :]
        old_acc, old_jerk = picked[14:17, :], picked[17:20, :]
        gone = now - picked[20:21, :]
        new_vel = old_vel + 0.5 * gone * (old_acc + force) + gone * gone / 12.0 * (old_jerk - jerk)
        new_pos = old_pos + 0.5 * gone * (old_vel + new_vel) + gone * gone / 12.0 * (old_acc - force)
        picked[0:3, :] = new_pos
        picked[3:6, :] = new_vel
        picked[6:9, :] = force
        picked[9:12, :] = jerk
        picked[12:13, :] = jnp.full((1, slots), now, F32)
        picked[13:14, :] = jnp.ones((1, slots), F32)
        picked[14:16, :] = jnp.zeros((2, slots), F32)
        live = lax.broadcasted_iota(jnp.int32, (1, slots), 1) < counts[step, me]
        pieces = jnp.concatenate(split3(jnp.where(live, picked[0:16, :], 0.0)), axis=0).astype(BF16)
        spread = lax.dot_general(pieces, chosen, NT, preferred_element_type=F32)
        spread = spread[0:16] + (spread[16:32] + spread[32:48])
        state[...] = jnp.where(spread[13:14] > 0.5, spread, state[...])
        return carry

    lax.fori_loop(0, steps, one_step, 0)
    out_pos[...] = state[0:3, :]
    out_vel[...] = state[3:6, :]
    out_acc[...] = state[6:9, :]
    out_jerk[...] = state[9:12, :]


def shards(groups, peers, positions, velocities, accelerations, jerks, levels, counts, active_rows):
    stars = positions.shape[1]
    steps, slots = active_rows.shape
    everyone = groups * peers
    stars_all = stars * everyone
    sends = (groups - 1) + groups * (peers - 1)
    vmem = pl.BlockSpec(memory_space=pltpu.VMEM)
    pairs_all = steps * slots * stars_all
    return pl.pallas_call(
        functools.partial(
            kernel,
            groups,
            peers,
            steps,
            0.0004 * (131072.0 / stars_all) ** (2.0 / 3.0),
            1.0 / stars_all,
        ),
        out_shape=[jax.ShapeDtypeStruct((3, stars), F32)] * 4,
        in_specs=[vmem] * 5 + [pl.BlockSpec(memory_space=pltpu.SMEM), vmem],
        out_specs=[vmem] * 4,
        scratch_shapes=[
            pltpu.VMEM((steps, everyone, 8, stars), F32),
            pltpu.VMEM((16, stars), F32),
            pltpu.VMEM((24, slots), F32),
            pltpu.VMEM((slots, 48), BF16),
            pltpu.VMEM((4, slots, 128), F32),
            pltpu.VMEM((4, slots, COLS), BF16),
            pltpu.VMEM((64, slots), F32),
            pltpu.SemaphoreType.DMA((steps, sends)),
            pltpu.SemaphoreType.DMA((steps, everyone)),
        ],
        compiler_params=pltpu.CompilerParams(
            collective_id=0, has_side_effects=True, vmem_limit_bytes=32 * 1024 * 1024
        ),
        cost_estimate=pl.CostEstimate(
            flops=40 * pairs_all, bytes_accessed=64 * stars, transcendentals=pairs_all
        ),
    )(positions, velocities, accelerations, jerks, levels[None, :], counts, active_rows)


def solution(mesh):
    split = P(None, ("grp", "dev"))
    return jax.shard_map(
        functools.partial(shards, mesh.shape["grp"], mesh.shape["dev"]),
        mesh=mesh,
        in_specs=(split, split, split, split, P(("grp", "dev")), P(), split),
        out_specs=(split, split, split, split),
        check_vma=False,
    )
```

time: 501 us -> 122 us (0.24)
  waiting for transfers between devices: 231 us -> 0 us
  other arithmetic: 135 us -> 0 us
  Pallas kernels: 0 us -> 113 us
  blocking collectives: 84.4 us -> 0 us
  local copies, waits for them, and re-layouts: 35.3 us -> 7.33 us
  between operations: 14.4 us -> 0.66 us
    psum x2 -> x0, waiting for transfers between devices: 231 us -> none  [shards(): totals = lax.psum(terms, ('grp', 'dev'))]
    reduce_sum x8 -> x0, other arithmetic: 129 us -> none  [pair_block(): jnp.sum(weight * (drift_z - along * gap_z), axis=1)]
    pallas_call x0 -> x1, Pallas kernels: none -> 113 us  [shards(): pl.pallas_call(functools.partial(kernel, groups, peers, steps, 0.0004 * (...]
    all_gather x2 -> x0, blocking collectives: 84.4 us -> none  [shards(): gathered = lax.all_gather(targets[None], ('grp', 'dev'), axis=0, tiled=True)]
    gather x26 -> x0, local copies, waits for them, and re-layouts: 12.5 us -> none  [the longest x8 3.27 us: shards(): targets = jnp.concatenate([pred_pos[:, rows], pred_vel[:, rows]], axis=0)]
    scatter x9 -> x0, local copies, waits for them, and re-layouts: 12.4 us -> none  [the longest x2 2.74 us: shards(): velocities = velocities.at[:, target].set(new_vel, mode='drop')]
  transfers between devices with their start and end apart: 2 -> 0, of which waited for: 2 -> 0; matrix products, arithmetic and copies ran while one was open for 2% -> 0% of each run, Pallas kernels for 0% -> 0%
where the time goes in v1:
time: 122 us; the launch traced here: 121 us
  Pallas kernels  113 us (93%)
  local copies, waits for them, and re-layouts  7.33 us (6%)
    pallas_call x1, Pallas kernels, shards(): pl.pallas_call(functools.partial(kernel, groups, peers, steps, 0.0004 * (...  113 us
    unnamed x18, local copies, waits for them, and re-layouts  7.33 us

profile of v1, /device:TPU:0, one launch (start us, length us, event | category | flops | bytes accessed | tf_op | source)
XLA Modules:
  0.0 121.0 jit_solution(11026502156999980120)
XLA Ops:
  0.6 0.0 copy-start.6
  0.6 0.7 copy-done.6
  1.3 0.0 copy-start
  1.3 0.7 copy-done
  2.0 0.0 copy-start.1
  2.0 0.7 copy-done.1
  2.7 0.0 copy-start.2
  2.8 0.7 copy-done.2
  3.5 0.0 copy-start.3
  3.5 0.7 copy-done.3
  4.2 0.0 copy-start.4
  4.2 0.7 copy-done.4
  4.9 0.0 copy-start.5
  4.9 0.7 copy-done.5
  5.6 113.1 %shard_map.102 = (f32[3,1024]{1,0:T(4,128)S(1)}, f32[3,1024]{1,0:T(4,128)S(1)}, f32[3,1024]{1,0:T(4,128)S(1)}, f32[3,1024]{1,0:T(4,128)S(1)}) custom-call(f32[3,1024]{1,0:T(4,128)S(1)} %copy-done, f32[3,1024]{1,0:T(4,128)S(1)} %copy-done.1, f32[3,1024]{1,0:T(4,128)S(1)} %copy-done.2, f32[3,1024]{1,0:T(4,128)S(1)} %copy-done.3, s32[1,1024]{1,0:T(1,128)S(1)} %bitcast.1, ...), custom_call_target="tpu_custom_call" | custom-call | flops 671088640 | bytes 65536 | tf_op jit(solution)/shard_map/pallas_call | solution.py:243
  118.6 0.6 copy.15
  119.2 0.6 copy.16
  119.8 0.6 copy.17
  120.4 0.6 copy.18
Async XLA Ops:
  0.6 0.7 copy-start.6
  1.3 0.7 copy-start
  2.0 0.7 copy-start.1
  2.7 0.7 copy-start.2
  3.5 0.7 copy-start.3
  4.2 0.7 copy-start.4
  4.9 0.7 copy-start.5

commit v2 on v1

--- a/solution.py
+++ b/solution.py
@@ -9,7 +9,6 @@
 
 tick_length = 1.0 / 128.0
 COLS = 256
-ROWS = 128
 F32 = jnp.float32
 BF16 = jnp.bfloat16
 NT = (((1,), (1,)), ((), ()))
@@ -22,37 +21,41 @@
     return high, middle, rest - middle
 
 
-def accumulate(chunk, width, slots, left_ref, place_ref, pairs_ref, total_ref):
+def accumulate(chunk, width, left_ref, place_ref, total_ref):
+    high, middle, low = split3(chunk)
+    right = jnp.concatenate([high, high, high, middle, middle, low], axis=0).astype(BF16)
+    parts = jnp.concatenate([high, middle, low, jnp.zeros_like(low)], axis=0).astype(BF16)
+    direct = total_ref[0:32, :]
+    turned = total_ref[32:64, :]
     for start in range(0, width, COLS):
-        source = chunk[:, start : start + COLS]
-        high, middle, low = split3(source)
-        right = jnp.concatenate([high, high, high, middle, middle, low], axis=0).astype(BF16)
-        parts = jnp.concatenate([high, middle, low, jnp.zeros_like(low)], axis=0).astype(BF16)
-        for row in range(0, slots, ROWS):
-            rows = slice(row, row + ROWS)
-            mixed = jnp.dot(left_ref[rows, :], right, preferred_element_type=F32)
-            for lane in range(0, COLS, 128):
-                lanes = slice(lane, lane + 128)
-                gap_x = source[0:1, lanes] - place_ref[0, rows, :]
-                gap_y = source[1:2, lanes] - place_ref[1, rows, :]
-                gap_z = source[2:3, lanes] - place_ref[2, rows, :]
-                squared = gap_x * gap_x + gap_y * gap_y + gap_z * gap_z + place_ref[3, 0:1, :]
-                inverse = lax.rsqrt(squared)
-                twice = inverse * inverse
-                weight = twice * inverse
-                along = weight * twice * mixed[:, lanes]
-                weight_high = weight.astype(BF16)
-                along_high = along.astype(BF16)
-                pairs_ref[0, rows, lanes] = weight_high
-                pairs_ref[1, rows, lanes] = (weight - weight_high.astype(F32)).astype(BF16)
-                pairs_ref[2, rows, lanes] = along_high
-                pairs_ref[3, rows, lanes] = (along - along_high.astype(F32)).astype(BF16)
-        total_ref[0:32, :] += lax.dot_general(
-            parts, pairs_ref[0], NT, preferred_element_type=F32
-        ) + lax.dot_general(parts, pairs_ref[1], NT, preferred_element_type=F32)
-        total_ref[32:64, :] += lax.dot_general(
-            parts, pairs_ref[2], NT, preferred_element_type=F32
-        ) + lax.dot_general(parts, pairs_ref[3], NT, preferred_element_type=F32)
+        columns = slice(start, start + COLS)
+        mixed = jnp.dot(left_ref[...], right[:, columns], preferred_element_type=F32)
+        pieces = [[], [], [], []]
+        for lane in range(0, COLS, 128):
+            lanes = slice(start + lane, start + lane + 128)
+            gap_x = chunk[0:1, lanes] - place_ref[0]
+            gap_y = chunk[1:2, lanes] - place_ref[1]
+            gap_z = chunk[2:3, lanes] - place_ref[2]
+            squared = gap_x * gap_x + gap_y * gap_y + gap_z * gap_z + place_ref[3, 0:1, :]
+            inverse = lax.rsqrt(squared)
+            twice = inverse * inverse
+            weight = twice * inverse
+            along = weight * twice * mixed[:, lane : lane + 128]
+            weight_high = weight.astype(BF16)
+            along_high = along.astype(BF16)
+            pieces[0].append(weight_high)
+            pieces[1].append((weight - weight_high.astype(F32)).astype(BF16))
+            pieces[2].append(along_high)
+            pieces[3].append((along - along_high.astype(F32)).astype(BF16))
+        part = parts[:, columns]
+        sums = [
+            lax.dot_general(part, jnp.concatenate(piece, axis=1), NT, preferred_element_type=F32)
+            for piece in pieces
+        ]
+        direct = direct + sums[0] + sums[1]
+        turned = turned + sums[2] + sums[3]
+    total_ref[0:32, :] = direct
+    total_ref[32:64, :] = turned
 
 
 def kernel(
@@ -77,7 +80,6 @@
     picked,
     left,
     place,
-    pairs,
     total,
     send_sem,
     recv_sem,
@@ -187,7 +189,7 @@
             def _():
                 send(step, owner, 0, (grp, lax.rem(dev + 1, peers))).wait_recv()
 
-            accumulate(held[step, owner], stars, slots, left, place, pairs, total)
+            accumulate(held[step, owner], stars, left, place, total)
             return inner
 
         lax.fori_loop(0, groups * peers, one_chunk, 0)
@@ -258,7 +260,6 @@
             pltpu.VMEM((24, slots), F32),
             pltpu.VMEM((slots, 48), BF16),
             pltpu.VMEM((4, slots, 128), F32),
-            pltpu.VMEM((4, slots, COLS), BF16),
             pltpu.VMEM((64, slots), F32),
             pltpu.SemaphoreType.DMA((steps, sends)),
             pltpu.SemaphoreType.DMA((steps, everyone)),

time: 122 us -> 90.9 us (0.75)
  Pallas kernels: 113 us -> 82.3 us
    pallas_call x1, Pallas kernels: 113 us -> 82.3 us  [shards(): pl.pallas_call(functools.partial(kernel, groups, peers, steps, 0.0004 * (...]
where the time goes in v2:
time: 90.9 us; the launch traced here: 90.3 us
  Pallas kernels  82.3 us (91%)
  local copies, waits for them, and re-layouts  7.33 us (8%)
    pallas_call x1, Pallas kernels, shards(): pl.pallas_call(functools.partial(kernel, groups, peers, steps, 0.0004 * (...  82.3 us
    unnamed x18, local copies, waits for them, and re-layouts  7.33 us

profile of v2, /device:TPU:0, one launch (start us, length us, event | category | flops | bytes accessed | tf_op | source)
XLA Modules:
  0.0 90.3 jit_solution(7762681140350243935)
XLA Ops:
  0.6 0.0 copy-start.6
  0.6 0.7 copy-done.6
  1.3 0.0 copy-start
  1.3 0.7 copy-done
  2.0 0.0 copy-start.1
  2.0 0.7 copy-done.1
  2.7 0.0 copy-start.2
  2.8 0.7 copy-done.2
  3.5 0.0 copy-start.3
  3.5 0.7 copy-done.3
  4.2 0.0 copy-start.4
  4.2 0.7 copy-done.4
  4.9 0.0 copy-start.5
  4.9 0.7 copy-done.5
  5.6 82.3 %shard_map.102 = (f32[3,1024]{1,0:T(4,128)S(1)}, f32[3,1024]{1,0:T(4,128)S(1)}, f32[3,1024]{1,0:T(4,128)S(1)}, f32[3,1024]{1,0:T(4,128)S(1)}) custom-call(f32[3,1024]{1,0:T(4,128)S(1)} %copy-done, f32[3,1024]{1,0:T(4,128)S(1)} %copy-done.1, f32[3,1024]{1,0:T(4,128)S(1)} %copy-done.2, f32[3,1024]{1,0:T(4,128)S(1)} %copy-done.3, s32[1,1024]{1,0:T(1,128)S(1)} %bitcast.1, ...), custom_call_target="tpu_custom_call" | custom-call | flops 671088640 | bytes 65536 | tf_op jit(solution)/shard_map/pallas_call | solution.py:245
  87.9 0.6 copy.15
  88.5 0.6 copy.16
  89.1 0.6 copy.17
  89.7 0.6 copy.18
Async XLA Ops:
  0.6 0.7 copy-start.6
  1.3 0.7 copy-start
  2.0 0.7 copy-start.1
  2.7 0.7 copy-start.2
  3.5 0.7 copy-start.3
  4.2 0.7 copy-start.4
  4.9 0.7 copy-start.5

commit v3 on v2

--- a/solution.py
+++ b/solution.py
@@ -21,12 +21,18 @@
     return high, middle, rest - middle
 
 
+def add_block(direct, turned, part, pieces):
+    sums = [lax.dot_general(part, piece, NT, preferred_element_type=F32) for piece in pieces]
+    return direct + sums[0] + sums[1], turned + sums[2] + sums[3]
+
+
 def accumulate(chunk, width, left_ref, place_ref, total_ref):
     high, middle, low = split3(chunk)
     right = jnp.concatenate([high, high, high, middle, middle, low], axis=0).astype(BF16)
     parts = jnp.concatenate([high, middle, low, jnp.zeros_like(low)], axis=0).astype(BF16)
     direct = total_ref[0:32, :]
     turned = total_ref[32:64, :]
+    ready = []
     for start in range(0, width, COLS):
         columns = slice(start, start + COLS)
         mixed = jnp.dot(left_ref[...], right[:, columns], preferred_element_type=F32)
@@ -47,13 +53,10 @@
             pieces[1].append((weight - weight_high.astype(F32)).astype(BF16))
             pieces[2].append(along_high)
             pieces[3].append((along - along_high.astype(F32)).astype(BF16))
-        part = parts[:, columns]
-        sums = [
-            lax.dot_general(part, jnp.concatenate(piece, axis=1), NT, preferred_element_type=F32)
-            for piece in pieces
-        ]
-        direct = direct + sums[0] + sums[1]
-        turned = turned + sums[2] + sums[3]
+        ready.append((parts[:, columns], [jnp.concatenate(piece, axis=1) for piece in pieces]))
+        if len(ready) > 1:
+            direct, turned = add_block(direct, turned, *ready.pop(0))
+    direct, turned = add_block(direct, turned, *ready.pop(0))
     total_ref[0:32, :] = direct
     total_ref[32:64, :] = turned
 

time: 90.9 us -> 85 us (0.935)
  Pallas kernels: 82.3 us -> 76.4 us
    pallas_call x1, Pallas kernels: 82.3 us -> 76.4 us  [shards(): pl.pallas_call(functools.partial(kernel, groups, peers, steps, 0.0004 * (...]
where the time goes in v3:
time: 85 us; the launch traced here: 84.4 us
  Pallas kernels  76.4 us (90%)
  local copies, waits for them, and re-layouts  7.33 us (9%)
    pallas_call x1, Pallas kernels, shards(): pl.pallas_call(functools.partial(kernel, groups, peers, steps, 0.0004 * (...  76.4 us
    unnamed x18, local copies, waits for them, and re-layouts  7.33 us

profile of v3, /device:TPU:0, one launch (start us, length us, event | category | flops | bytes accessed | tf_op | source)
XLA Modules:
  0.0 84.4 jit_solution(2534131303876616252)
XLA Ops:
  0.6 0.0 copy-start.6
  0.6 0.7 copy-done.6
  1.3 0.0 copy-start
  1.3 0.7 copy-done
  2.0 0.0 copy-start.1
  2.0 0.7 copy-done.1
  2.7 0.0 copy-start.2
  2.8 0.7 copy-done.2
  3.5 0.0 copy-start.3
  3.5 0.7 copy-done.3
  4.2 0.0 copy-start.4
  4.2 0.7 copy-done.4
  4.9 0.0 copy-start.5
  4.9 0.7 copy-done.5
  5.6 76.4 %shard_map.102 = (f32[3,1024]{1,0:T(4,128)S(1)}, f32[3,1024]{1,0:T(4,128)S(1)}, f32[3,1024]{1,0:T(4,128)S(1)}, f32[3,1024]{1,0:T(4,128)S(1)}) custom-call(f32[3,1024]{1,0:T(4,128)S(1)} %copy-done, f32[3,1024]{1,0:T(4,128)S(1)} %copy-done.1, f32[3,1024]{1,0:T(4,128)S(1)} %copy-done.2, f32[3,1024]{1,0:T(4,128)S(1)} %copy-done.3, s32[1,1024]{1,0:T(1,128)S(1)} %bitcast.1, ...), custom_call_target="tpu_custom_call" | custom-call | flops 671088640 | bytes 65536 | tf_op jit(solution)/shard_map/pallas_call | solution.py:248
  82.0 0.6 copy.15
  82.6 0.6 copy.16
  83.2 0.6 copy.17
  83.8 0.6 copy.18
Async XLA Ops:
  0.6 0.7 copy-start.6
  1.3 0.7 copy-start
  2.0 0.7 copy-start.1
  2.7 0.7 copy-start.2
  3.5 0.7 copy-start.3
  4.2 0.7 copy-start.4
  4.9 0.7 copy-start.5
